TPU v7x, 32 devices: a whole 2x2x4 slice. The times are simulated.
32 devices in a mesh: grp: 2 (over y), seq: 4 (over z), smp: 2 (over x), rep: 2 (over core).
Axes of the slice: x: 2, y: 2, z: 4, core: 2. Of those that a mesh axis runs over, the one named last changes fastest.
Arguments:
- atom_single: bfloat16 [32, 512, 128], P(('grp', 'smp', 'rep'), 'seq'), parts along dimension 0, may hold values from -6 to 6
- token_counts: int32 [8, 16], P(('grp', 'seq')), parts along dimension 0, may hold values from 1 to 24, 128 in all within a row
- key_shift: int32 [32], P(('grp', 'seq')), parts along dimension 0, may hold values from -16 to 16, as said below
- atom_pair: bfloat16 [32, 16, 4096], P(('grp', 'seq')), parts along dimension 0, may hold values from -500 to 500
- project_weight: bfloat16 [4, 128, 128], replicated, may hold values from -0.5 to 0.5
- bias_weight: float32 [16, 4], replicated, may hold values from -1.5 to 1.5
- output_weight: bfloat16 [128, 128], replicated, may hold values from -0.5 to 0.5
- token_weight: bfloat16 [128, 768], replicated, may hold values from -0.5 to 0.5
- token_grad: bfloat16 [32, 64, 768], P(('grp', 'smp', 'rep'), 'seq'), parts along dimension 0, may hold values from -24 to 24
Outputs:
- single_grad: bfloat16 [32, 512, 128], P(('grp', 'smp', 'rep'), 'seq'), parts along dimension 0
- pair_grad: bfloat16 [32, 16, 4096], P(('grp', 'seq'), None, ('smp', 'rep')), parts along dimension 0
- token_weight_grad: float32 [256, 768], P('grp'), parts along dimension 0
- project_weight_grad: float32 [8, 128, 128], P('grp'), parts along dimension 0
There are 2 independent parts, one for each index of `grp`. A program takes and returns all parts, laid end to end along the dimension named above; an argument that names none is the same for every part. Nothing has to cross between parts.
Inputs may be any that keep to these rules, and one draw needn't show every extreme that they name: `token_counts`: each row of 16 counts sums to 128: the atoms of a block of 128 atoms belong to the tokens of the same block, in token order. `key_shift`: each value is -16, 0 or 16; the first window's is -16 and the last window's is 16.
All inputs are finite; a program needn't handle non-finite values.
Results may differ from a plain program's by a relative error of at most 0.02.
Values may be sent and summed in bfloat16 or wider, within the bound.
A program may use at most 64 MiB of HBM per device.

v0:
```python
import jax
import jax.numpy as jnp
from jax import lax
from jax.sharding import PartitionSpec as P

H = 4
HD = 32
QW = 32
KW = 128
HALO = 64


EPSILON = 1e-05


def padded(array, sides, width):
    for axis, dim in sides:
        devices, length = (lax.axis_size(axis), array.shape[dim])
        up = [(i, (i + 1) % devices) for i in range(devices - 1)]
        down = [(j, i) for i, j in up]
        last = lax.slice_in_dim(array, length - width, length, axis=dim)
        initial = lax.slice_in_dim(array, 0, width, axis=dim)
        before = lax.ppermute(last, axis, up)
        after = lax.ppermute(initial, axis, down)
        array = jnp.concatenate([before, array, after], axis=dim)
    return array


def from_behind(value, axis, steps):
    count = lax.axis_size(axis)
    initial, last = (max(0, -steps), min(count, count - steps))
    return lax.ppermute(value, axis, [(source, source + steps) for source in range(initial, last)])


def layer_norm(values):
    center = values - jnp.mean(values, axis=-1, keepdims=True)
    variance = jnp.mean(center * center, axis=-1, keepdims=True)
    inverse = 1.0 / jnp.sqrt(variance + EPSILON)
    return (center * inverse, inverse)


def silu_slope(preact):
    sigma = jax.nn.sigmoid(preact)
    return sigma * (1.0 + preact * (1.0 - sigma))


def on_device(
    atom_single,
    token_counts,
    key_shift,
    atom_pair,
    project_weight,
    bias_weight,
    output_weight,
    token_weight,
    token_grad,
):
    samples, atoms, width = atom_single.shape
    windows = key_shift.shape[0]
    heads_width = H * HD
    score_scale = HD ** (-0.5)
    single32 = atom_single.astype(jnp.float32)
    normed, inverse = layer_norm(single32)
    normed_half = normed.astype(jnp.bfloat16)
    projected = jnp.einsum(
        "sac,kcd->ksad", normed_half, project_weight, preferred_element_type=jnp.float32
    )
    queries = projected[0].astype(jnp.bfloat16)
    gate = jax.nn.sigmoid(projected[3])
    own_pairs = jnp.concatenate([projected[1], projected[2]], axis=-1).astype(jnp.bfloat16)
    extended = padded(own_pairs, (("seq", 1),), HALO)
    device = lax.axis_index("seq")
    total_atoms = lax.axis_size("seq") * atoms
    window_ids = jnp.arange(windows, dtype=jnp.int32)
    begin_at = QW * window_ids - (KW - QW) // 2 + key_shift + HALO
    key_global = (
        device * atoms + begin_at[:, None] - HALO + jnp.arange(KW, dtype=jnp.int32)[None, :]
    )
    key_valid = (key_global >= 0) & (key_global < total_atoms)
    gathered = jax.vmap(lambda start: lax.dynamic_slice_in_dim(extended, start, KW, axis=1))(
        begin_at
    )
    key_win = gathered[..., :heads_width].reshape(windows, samples, KW, H, HD)
    value_win = gathered[..., heads_width:].reshape(windows, samples, KW, H, HD)
    query_win = queries.reshape(samples, windows, QW, H, HD)
    bias = jnp.einsum(
        "wci,ch->whi", atom_pair.astype(jnp.float32), bias_weight, precision=lax.Precision.HIGHEST
    ).reshape(windows, H, QW, KW)
    scores = (
        jnp.einsum("swqhd,wskhd->swhqk", query_win, key_win, preferred_element_type=jnp.float32)
        * score_scale
        + bias[None]
    )
    scores = jnp.where(key_valid[None, :, None, None, :], scores, -jnp.inf)
    row_top = jnp.max(scores, axis=-1, keepdims=True)
    expo = jnp.exp(scores - row_top)
    probs = expo / jnp.sum(expo, axis=-1, keepdims=True)
    probs_half = probs.astype(jnp.bfloat16)
    attended = jnp.einsum(
        "swhqk,wskhd->swqhd", probs_half, value_win, preferred_element_type=jnp.float32
    ).reshape(samples, atoms, heads_width)
    gated = (gate * attended).astype(jnp.bfloat16)
    hidden = (
        single32
        + jnp.einsum("sad,dc->sac", gated, output_weight, preferred_element_type=jnp.float32)
    ).astype(jnp.bfloat16)
    preact = jnp.einsum("sac,ct->sat", hidden, token_weight, preferred_element_type=jnp.float32)
    counts_row = token_counts[0]
    token_ends = jnp.cumsum(counts_row)
    token_begins = token_ends - counts_row
    positions = jnp.arange(atoms, dtype=jnp.int32)[:, None]
    member = (positions >= token_begins[None, :]) & (positions < token_ends[None, :])
    atom_count = jnp.sum(jnp.where(member, counts_row[None, :], 0), axis=1).astype(jnp.float32)
    picked = (
        jnp.einsum(
            "at,stc->sac",
            member.astype(jnp.bfloat16),
            token_grad,
            preferred_element_type=jnp.float32,
        )
        / atom_count[None, :, None]
    )
    slope_grad = (picked * silu_slope(preact)).astype(jnp.bfloat16)
    token_part = jnp.einsum("sac,sat->ct", hidden, slope_grad, preferred_element_type=jnp.float32)
    hidden_grad = jnp.einsum(
        "sat,ct->sac", slope_grad, token_weight, preferred_element_type=jnp.float32
    )
    hidden_half = hidden_grad.astype(jnp.bfloat16)
    gated_grad = jnp.einsum(
        "sac,dc->sad", hidden_half, output_weight, preferred_element_type=jnp.float32
    )
    attended_grad = (gated_grad * gate).astype(jnp.bfloat16)
    gate_grad = (gated_grad * attended * gate * (1.0 - gate)).astype(jnp.bfloat16)
    attended_win = attended_grad.reshape(samples, windows, QW, H, HD)
    prob_grad = jnp.einsum(
        "swqhd,wskhd->swhqk", attended_win, value_win, preferred_element_type=jnp.float32
    )
    row_total = jnp.sum(probs * prob_grad, axis=-1, keepdims=True)
    logit_grad = probs * (prob_grad - row_total)
    logit_half = logit_grad.astype(jnp.bfloat16)
    query_grad = (
        (
            jnp.einsum(
                "swhqk,wskhd->swqhd", logit_half, key_win, preferred_element_type=jnp.float32
            )
            * score_scale
        )
        .reshape(samples, atoms, heads_width)
        .astype(jnp.bfloat16)
    )
    key_grad_win = (
        jnp.einsum("swhqk,swqhd->wskhd", logit_half, query_win, preferred_element_type=jnp.float32)
        * score_scale
    )
    value_grad_win = jnp.einsum(
        "swhqk,swqhd->wskhd", probs_half, attended_win, preferred_element_type=jnp.float32
    )
    combined = jnp.concatenate(
        [
            key_grad_win.reshape(windows, samples, KW, heads_width),
            value_grad_win.reshape(windows, samples, KW, heads_width),
        ],
        axis=-1,
    )

    def scatter_window(window, total):
        start = begin_at[window]
        current = lax.dynamic_slice_in_dim(total, start, KW, axis=1)
        return lax.dynamic_update_slice_in_dim(total, current + combined[window], start, axis=1)

    accumulated = lax.fori_loop(
        0,
        windows,
        scatter_window,
        jnp.zeros((samples, atoms + 2 * HALO, 2 * heads_width), jnp.float32),
    )
    from_right = from_behind(accumulated[:, :HALO].astype(jnp.bfloat16), "seq", -1).astype(
        jnp.float32
    )
    from_left = from_behind(accumulated[:, HALO + atoms :].astype(jnp.bfloat16), "seq", 1).astype(
        jnp.float32
    )
    own_total = (
        accumulated[:, HALO : HALO + atoms]
        + jnp.pad(from_left, ((0, 0), (0, atoms - HALO), (0, 0)))
        + jnp.pad(from_right, ((0, 0), (atoms - HALO, 0), (0, 0)))
    )
    key_grad = own_total[..., :heads_width].astype(jnp.bfloat16)
    value_grad = own_total[..., heads_width:].astype(jnp.bfloat16)
    stacked = jnp.stack([query_grad, key_grad, value_grad, gate_grad])
    project_part = jnp.einsum(
        "sac,ksad->kcd", normed_half, stacked, preferred_element_type=jnp.float32
    )
    normed_grad = jnp.einsum(
        "ksad,kcd->sac", stacked, project_weight, preferred_element_type=jnp.float32
    )
    ln_grad = inverse * (
        normed_grad
        - jnp.mean(normed_grad, axis=-1, keepdims=True)
        - normed * jnp.mean(normed_grad * normed, axis=-1, keepdims=True)
    )
    single_grad = (hidden_grad + ln_grad).astype(jnp.bfloat16)
    token_total, project_total = lax.psum((token_part, project_part), ("seq", "smp", "rep"))
    logit_flat = logit_grad.reshape(samples, windows, H, QW * KW)
    pair_part = jnp.einsum("swhi,ch->wci", logit_flat, bias_weight, precision=lax.Precision.HIGHEST)
    pair_grad = lax.psum_scatter(
        pair_part.astype(jnp.bfloat16), ("smp", "rep"), scatter_dimension=2, tiled=True
    )
    return (single_grad, pair_grad, token_total, project_total)


def solution(mesh):
    in_specs = (
        P(("grp", "smp", "rep"), "seq", None),
        P(("grp", "seq"), None),
        P(("grp", "seq")),
        P(("grp", "seq"), None, None),
        P(),
        P(),
        P(),
        P(),
        P(("grp", "smp", "rep"), "seq", None),
    )
    out_specs = (
        P(("grp", "smp", "rep"), "seq", None),
        P(("grp", "seq"), None, ("smp", "rep")),
        P("grp", None),
        P("grp", None, None),
    )
    return jax.shard_map(
        on_device, mesh=mesh, in_specs=in_specs, out_specs=out_specs, check_vma=False
    )
```

profile of v0, /device:TPU:0, one launch (start us, length us, event | category | flops | bytes accessed | tf_op | source)
XLA Modules:
  0.0 199.3 jit_solution(6640250450622201787)
XLA Ops:
  9.1 1.1 fusion.30
  10.3 2.4 %fusion.70 = (bf16[4,4,128,128]{2,3,0,1:T(8,128)(2,1)S(1)}, f32[4,4,128,128]{2,3,0,1:T(8,128)}) fusion(bf16[4,128,128]{2,1,0:T(8,128)(2,1)} %param.15, f32[4,128]{1,0:T(4,128)S(1)} %add_rsqrt_fusion, f32[4,128]{1,0:T(4,128)S(1)} %broadcast_multiply_fusion.2, bf16[4,128,128]{2,1,0:T(8,128)(2,1)} %param.11), kind=kOutput, calls=%fused_computation.113 | convolution fusion | flops 67633152 | bytes 1839104 | tf_op jit(solution)/shard_map/sac,kcd->ksad/dot_general | solution.py:65
  12.9 4.9 %collective-permute-start = (bf16[4,64,256]{1,2,0:T(8,128)(2,1)S(1)}, bf16[4,64,256]{1,2,0:T(8,128)(2,1)S(1)}, u32[]{:S(2)}, u32[]{:S(2)}) collective-permute-start(bf16[4,64,256]{1,2,0:T(8,128)(2,1)S(1)} %get-tuple-element.115), channel_id=1, source_target_pairs={{0,4},{4,8},{8,12},{1,5},{5,9},{9,13},{2,6},{6,10},{10,14},{3,7},{... | collective-permute-start | bytes 393224 | tf_op jit(solution)/shard_map/ppermute | solution.py:23
  17.9 1.3 collective-permute-start.1
  20.3 1.7 fusion.50
  23.4 4.1 %collective-permute-done.1 = bf16[4,64,256]{1,2,0:T(8,128)(2,1)S(1)} collective-permute-done((bf16[4,64,256]{1,2,0:T(8,128)(2,1)S(1)}, bf16[4,64,256]{1,2,0:T(8,128)(2,1)S(1)}, u32[]{:S(2)}, u32[]{:S(2)}) %collective-permute-start.1) | collective-permute-done | bytes 131104 | tf_op jit(solution)/shard_map/ppermute | solution.py:24
  28.2 1.4 gather_fusion
  34.4 1.2 fusion.9
  35.6 2.2 %fusion.2 = bf16[4,128,768]{2,1,0:T(8,128)(2,1)S(1)} fusion(f32[128,4,768]{2,0,1:T(8,128)} %fusion.50, bf16[4,128,128]{2,1,0:T(8,128)(2,1)S(1)} %fusion.9, f32[128]{0:T(128)S(1)} %copy-done.27, bf16[128,768]{1,0:T(8,128)(2,1)S(1)} %copy-done.12), kind=kOutput, calls=%fused_computation.9 | convolution fusion | flops 104595456 | bytes 2687488 | tf_op jit(solution)/shard_map/sac,ct->sat/dot_general | solution.py:107
  38.3 2.0 multiply_convert_fusion.1
  40.3 1.9 reshape.115
  42.2 2.0 %multiply_reduce_fusion = (f32[4,4,4,32]{3,2,1,0:T(4,128)S(1)}, f32[4,4,4,32,128]{4,3,2,1,0:T(8,128)S(1)}) fusion(f32[4,4,4,32,128]{4,3,2,1,0:T(8,128)S(1)} %copy-done.5, f32[4,4,4,32]{3,2,1,0:T(4,128)} %copy-done.20, bf16[4,4,128,4,32]{2,4,3,0,1:T(8,128)(2,1)} %bitcast.138, bf16[4,4,32,4,32]{2,1,4,3,0:T(4,128)(2,1)} %reshape.115), kind=kOutput, calls=%fused_computation.27 | convolution fusion | flops 17561600 | bytes 2768896 | tf_op jit(solution)/shard_map/swqhd,wskhd->swhqk/dot_general | solution.py:135
  44.3 1.6 fusion.18
  47.3 1.5 fusion.10
  50.4 1.6 copy.56
  52.0 1.5 pad_maximum_fusion
  53.6 27.4 %while.13 = (s32[]{:T(128)}, f32[4,256,256]{1,2,0:T(8,128)S(1)}, s32[4]{0:T(128)S(1)}, f32[4,4,128,256]{3,2,1,0:T(8,128)}, s32[]{:T(128)}, /*index=5*/s32[]{:T(128)}, s32[]{:T(128)}) while((s32[]{:T(128)}, f32[4,256,256]{1,2,0:T(8,128)S(1)}, s32[4]{0:T(128)S(1)}, f32[4,4,128,256]{3,2,1,0:T(8,128)}, s32[]{:T(128)}, /*index=5*/s32[]{:T(128)}, ...), condition=%wide.region_8.9_spmd, body=%wide.region_7.8_spmd.sunk | while | flops 131077 | bytes 5767303 | solution.py:171
  57.9 2.3 %dynamic_update_slice.8 = f32[4,256,256]{1,2,0:T(8,128)S(1)} dynamic-update-slice(f32[4,256,256]{1,2,0:T(8,128)S(1)} %get-tuple-element.163, f32[4,128,256]{1,2,0:T(8,128)S(1)} %copy.104, s32[]{:T(128)} %constant.65.clone.1..sunk, s32[]{:T(128)S(6)} %select_n.38, s32[]{:T(128)} %constant.65.clone.1..sunk) | dynamic-update-slice | bytes 1048580 | tf_op jit(solution)/shard_map/while/body/eval_jaxpr/dynamic_update_slice | solution.py:169
  64.4 3.3 %dynamic_update_slice.8 = f32[4,256,256]{1,2,0:T(8,128)S(1)} dynamic-update-slice(f32[4,256,256]{1,2,0:T(8,128)S(1)} %get-tuple-element.163, f32[4,128,256]{1,2,0:T(8,128)S(1)} %copy.104, s32[]{:T(128)} %constant.65.clone.1..sunk, s32[]{:T(128)S(6)} %select_n.38, s32[]{:T(128)} %constant.65.clone.1..sunk) | dynamic-update-slice | bytes 1048580 | tf_op jit(solution)/shard_map/while/body/eval_jaxpr/dynamic_update_slice | solution.py:169
  70.7 1.1 bitcast_add_fusion.2
  72.0 3.3 %dynamic_update_slice.8 = f32[4,256,256]{1,2,0:T(8,128)S(1)} dynamic-update-slice(f32[4,256,256]{1,2,0:T(8,128)S(1)} %get-tuple-element.163, f32[4,128,256]{1,2,0:T(8,128)S(1)} %copy.104, s32[]{:T(128)} %constant.65.clone.1..sunk, s32[]{:T(128)S(6)} %select_n.38, s32[]{:T(128)} %constant.65.clone.1..sunk) | dynamic-update-slice | bytes 1048580 | tf_op jit(solution)/shard_map/while/body/eval_jaxpr/dynamic_update_slice | solution.py:169
  78.2 1.1 bitcast_add_fusion.2
  79.6 1.4 dynamic_update_slice.8
  81.2 5.4 %collective-permute-start.2 = (bf16[4,64,256]{1,2,0:T(8,128)(2,1)S(1)}, bf16[4,64,256]{1,2,0:T(8,128)(2,1)S(1)}, u32[]{:S(2)}, u32[]{:S(2)}) collective-permute-start(bf16[4,64,256]{1,2,0:T(8,128)(2,1)S(1)} %get-tuple-element.108), channel_id=1, source_target_pairs={{0,4},{4,8},{8,12},{1,5},{5,9},{9,13},{2,6},{6,10},{10,14},{3,7},{... | collective-permute-start | bytes 393224 | tf_op jit(solution)/shard_map/ppermute | solution.py:32
  86.6 1.4 collective-permute-start.3
  89.1 1.8 collective-permute-done.2
  90.9 5.1 %collective-permute-done.3 = bf16[4,64,256]{1,2,0:T(8,128)(2,1)S(1)} collective-permute-done((bf16[4,64,256]{1,2,0:T(8,128)(2,1)S(1)}, bf16[4,64,256]{1,2,0:T(8,128)(2,1)S(1)}, u32[]{:S(2)}, u32[]{:S(2)}) %collective-permute-start.3) | collective-permute-done | bytes 131104 | tf_op jit(solution)/shard_map/ppermute | solution.py:32
  96.4 1.2 convolution_bitcast_fusion.5
  97.7 1.8 fusion.1
  101.6 86.7 %all-reduce.5.cloned.1.call-done = (f32[128,768]{1,0:T(8,128)}, f32[4,128,128]{1,2,0:T(8,128)}) async-done(((f32[128,768]{1,0:T(8,128)}, f32[4,128,128]{1,2,0:T(8,128)}), (f32[128,768]{1,0:T(8,128)}, f32[4,128,128]{1,2,0:T(8,128)})) %all-reduce.5.cloned.1.call-update) | async-done | bytes 655376 | tf_op jit(solution)/shard_map/psum | solution.py:203
  188.3 1.8 copy.64
  190.1 1.8 copy.114
  (127 shorter events, 23.1 us)
Async XLA Ops:
  8.0 11.4 %copy-start = (bf16[4,16,4096]{2,1,0:T(8,128)(2,1)S(1)}, bf16[4,16,4096]{2,1,0:T(8,128)(2,1)}, u32[]{:S(2)}) copy-start(bf16[4,16,4096]{2,1,0:T(8,128)(2,1)} %param.14) | copy-start | bytes 1572868
  8.0 180.3 %all-reduce.5.cloned.1.call-start = ((), (), s32[]{:S(2)}) async-start(), calls=%async_computation.2 | async-start | bytes 1310720 | tf_op jit(solution)/shard_map/psum | solution.py:203
  12.7 6.7 %copy-start.22 = (f32[16,4]{0,1:T(4,128)S(1)}, f32[16,4]{0,1:T(4,128)}, u32[]{:S(2)}) copy-start(f32[16,4]{0,1:T(4,128)} %param.16) | copy-start | bytes 772
  12.8 7.3 %copy-start.23 = (s32[1,16]{1,0:T(1,128)S(1)}, s32[1,16]{1,0:T(1,128)}, u32[]{:S(2)}) copy-start(s32[1,16]{1,0:T(1,128)} %param.12) | copy-start | bytes 196
  12.8 7.5 %copy-start.19 = (bf16[4,16,768]{2,1,0:T(8,128)(2,1)S(1)}, bf16[4,16,768]{2,1,0:T(8,128)(2,1)}, u32[]{:S(2)}) copy-start(bf16[4,16,768]{2,1,0:T(8,128)(2,1)} %param.19) | copy-start | bytes 294916
  12.9 10.5 %collective-permute-start = (bf16[4,64,256]{1,2,0:T(8,128)(2,1)S(1)}, bf16[4,64,256]{1,2,0:T(8,128)(2,1)S(1)}, u32[]{:S(2)}, u32[]{:S(2)}) collective-permute-start(bf16[4,64,256]{1,2,0:T(8,128)(2,1)S(1)} %get-tuple-element.115), channel_id=1, source_target_pairs={{0,4},{4,8},{8,12},{1,5},{5,9},{9,13},{2,6},{6,10},{10,14},{3,7},{... | collective-permute-start | bytes 393224 | tf_op jit(solution)/shard_map/ppermute | solution.py:23
  17.9 9.7 %collective-permute-start.1 = (bf16[4,64,256]{1,2,0:T(8,128)(2,1)S(1)}, bf16[4,64,256]{1,2,0:T(8,128)(2,1)S(1)}, u32[]{:S(2)}, u32[]{:S(2)}) collective-permute-start(bf16[4,64,256]{1,2,0:T(8,128)(2,1)S(1)} %get-tuple-element.116), channel_id=1, source_target_pairs={{4,0},{8,4},{12,8},{5,1},{9,5},{13,9},{6,2},{10,6},{14,10},{7,3},{... | collective-permute-start | bytes 393224 | tf_op jit(solution)/shard_map/ppermute | solution.py:24
  19.4 11.3 %copy-start.2 = (bf16[4,4,32,4,32]{2,1,4,3,0:T(4,128)(2,1)}, bf16[4,4,32,4,32]{2,1,4,3,0:T(4,128)(2,1)S(1)}, u32[]{:S(2)}) copy-start(bf16[4,4,32,4,32]{2,1,4,3,0:T(4,128)(2,1)S(1)} %convert_element_type.83) | copy-start | bytes 393220
  19.5 3.1 %copy-start.24 = (s32[4]{0:T(128)S(1)}, s32[4]{0:T(128)}, u32[]{:S(2)}) copy-start(s32[4]{0:T(128)} %param.13) | copy-start | bytes 52
  31.7 1.5 copy-start.20
  33.1 1.2 copy-start.1
  33.1 1.2 copy-start.25
  33.9 1.7 copy-start.12
  33.9 1.7 copy-start.27
  35.6 2.3 %copy-start.17 = (bf16[4,128,128]{2,1,0:T(8,128)(2,1)}, bf16[4,128,128]{2,1,0:T(8,128)(2,1)S(1)}, u32[]{:S(2)}) copy-start(bf16[4,128,128]{2,1,0:T(8,128)(2,1)S(1)} %fusion.9) | copy-start | bytes 393220
  35.6 2.3 %copy-start.13 = (bf16[128,768]{1,0:T(8,128)(2,1)S(1)}, bf16[128,768]{1,0:T(8,128)(2,1)}, u32[]{:S(2)}) copy-start(bf16[128,768]{1,0:T(8,128)(2,1)} %param.18) | copy-start | bytes 589828
  35.6 2.6 %copy-start.26 = (bf16[128,128]{1,0:T(8,128)(2,1)S(1)}, bf16[128,128]{1,0:T(8,128)(2,1)}, u32[]{:S(2)}) copy-start(bf16[128,128]{1,0:T(8,128)(2,1)} %param.17) | copy-start | bytes 98308
  37.9 4.3 %copy-start.5 = (f32[4,4,4,32,128]{4,3,2,1,0:T(8,128)S(1)}, f32[4,4,4,32,128]{4,3,2,1,0:T(8,128)}, u32[]{:S(2)}) copy-start(f32[4,4,4,32,128]{4,3,2,1,0:T(8,128)} %copy-done.4) | copy-start | bytes 3145732
  38.3 6.0 %copy-start.7 = (f32[4,128,128]{2,1,0:T(8,128)}, f32[4,128,128]{2,1,0:T(8,128)S(1)}, u32[]{:S(2)}) copy-start(f32[4,128,128]{2,1,0:T(8,128)S(1)} %fusion.35) | copy-start | bytes 786436
  42.2 2.1 %copy-start.21 = (f32[4,4,4,32]{3,2,1,0:T(4,128)S(1)}, f32[4,4,4,32]{3,2,1,0:T(4,128)}, u32[]{:S(2)}) copy-start(f32[4,4,4,32]{3,2,1,0:T(4,128)} %copy-done.20) | copy-start | bytes 24580
  44.3 2.0 %copy-start.3 = (bf16[4,4,32,4,32]{2,1,4,3,0:T(4,128)(2,1)S(1)}, bf16[4,4,32,4,32]{2,1,4,3,0:T(4,128)(2,1)}, u32[]{:S(2)}) copy-start(bf16[4,4,32,4,32]{2,1,4,3,0:T(4,128)(2,1)} %copy-done.2) | copy-start | bytes 393220
  45.9 1.4 copy-start.10
  81.0 7.1 %copy-start.18 = (bf16[4,128,128]{2,1,0:T(8,128)(2,1)S(1)}, bf16[4,128,128]{2,1,0:T(8,128)(2,1)}, u32[]{:S(2)}) copy-start(bf16[4,128,128]{2,1,0:T(8,128)(2,1)} %copy-done.17) | copy-start | bytes 393220
  81.2 9.7 %collective-permute-start.2 = (bf16[4,64,256]{1,2,0:T(8,128)(2,1)S(1)}, bf16[4,64,256]{1,2,0:T(8,128)(2,1)S(1)}, u32[]{:S(2)}, u32[]{:S(2)}) collective-permute-start(bf16[4,64,256]{1,2,0:T(8,128)(2,1)S(1)} %get-tuple-element.108), channel_id=1, source_target_pairs={{0,4},{4,8},{8,12},{1,5},{5,9},{9,13},{2,6},{6,10},{10,14},{3,7},{... | collective-permute-start | bytes 393224 | tf_op jit(solution)/shard_map/ppermute | solution.py:32
  86.6 9.8 %copy-start.15 = (bf16[1,4,128,128]{2,3,1,0:T(8,128)(2,1)S(1)}, bf16[1,4,128,128]{2,3,1,0:T(8,128)(2,1)}, u32[]{:S(2)}) copy-start(bf16[1,4,128,128]{2,3,1,0:T(8,128)(2,1)} %convert_element_type.93) | copy-start | bytes 393220
  86.6 9.8 %copy-start.28 = (bf16[1,4,128,128]{2,3,1,0:T(8,128)(2,1)S(1)}, bf16[1,4,128,128]{2,3,1,0:T(8,128)(2,1)}, u32[]{:S(2)}) copy-start(bf16[1,4,128,128]{2,3,1,0:T(8,128)(2,1)} %get-tuple-element.105) | copy-start | bytes 393220
  86.6 9.5 %collective-permute-start.3 = (bf16[4,64,256]{1,2,0:T(8,128)(2,1)S(1)}, bf16[4,64,256]{1,2,0:T(8,128)(2,1)S(1)}, u32[]{:S(2)}, u32[]{:S(2)}) collective-permute-start(bf16[4,64,256]{1,2,0:T(8,128)(2,1)S(1)} %get-tuple-element.109), channel_id=1, source_target_pairs={{4,0},{8,4},{12,8},{5,1},{9,5},{13,9},{6,2},{10,6},{14,10},{7,3},{... | collective-permute-start | bytes 393224 | tf_op jit(solution)/shard_map/ppermute | solution.py:32
  96.3 1.3 copy-start.9
  97.5 2.0 %copy-start.14 = (bf16[4,128,128]{2,1,0:T(8,128)(2,1)S(1)}, bf16[4,128,128]{2,1,0:T(8,128)(2,1)}, u32[]{:S(2)}) copy-start(bf16[4,128,128]{2,1,0:T(8,128)(2,1)} %param.15) | copy-start | bytes 393220
  97.5 2.0 %copy-start.16 = (bf16[1,4,128,128]{2,3,1,0:T(8,128)(2,1)S(1)}, bf16[1,4,128,128]{2,3,1,0:T(8,128)(2,1)}, u32[]{:S(2)}) copy-start(bf16[1,4,128,128]{2,3,1,0:T(8,128)(2,1)} %convert_element_type.93) | copy-start | bytes 393220
  97.5 2.1 %copy-start.29 = (bf16[1,4,128,128]{2,3,1,0:T(8,128)(2,1)S(1)}, bf16[1,4,128,128]{2,3,1,0:T(8,128)(2,1)}, u32[]{:S(2)}) copy-start(bf16[1,4,128,128]{2,3,1,0:T(8,128)(2,1)} %get-tuple-element.105) | copy-start | bytes 393220
  97.6 92.5 %reduce-scatter.2.cloned.1.call-start = ((), (), s32[]{:S(2)}) async-start(), calls=%async_computation.1 | async-start | bytes 655360 | tf_op jit(solution)/shard_map/reduce_scatter | solution.py:206
  (4 other events, 4.1 us)
Sparse Core Ops, SparseCore 0:
  97.7 90.5 all-reduce.4
Sparse Core Ops, SparseCore 1:
  101.1 20.9 reduce-scatter.1
where the time goes:
time: 200 us; the launch traced here: 199 us
  waiting for transfers between devices  98.6 us (49%)
  local copies, waits for them, and re-layouts  30.7 us (15%)
  matrix products  20 us (10%)
  between operations  16.1 us (8%)
  starting transfers between devices  13.1 us (7%)
  other arithmetic  12.8 us (6%)
  loops' own time  7.96 us (4%)
    psum x1, waiting for transfers between devices, on_device(): lax.psum((token_part, project_part), ('seq', 'smp', 'rep'))  86.7 us
    dynamic_update_slice x8, local copies, waits for them, and re-layouts, scatter_window(): lax.dynamic_update_slice_in_dim(total, current + combined[window], start,...  11 us
    another operation x1, loops' own time, on_device(): lax.fori_loop(0, windows, scatter_window, jnp.zeros((samples, atoms + 2 *...  7.96 us
    ppermute x2, waiting for transfers between devices, from_behind(): lax.ppermute(value, axis, [(source, source + steps) for source in range(i...  6.97 us
    ppermute x2, starting transfers between devices, from_behind(): lax.ppermute(value, axis, [(source, source + steps) for source in range(i...  6.81 us
    unnamed x62, local copies, waits for them, and re-layouts  5.57 us
    ppermute x1, starting transfers between devices, padded(): before = lax.ppermute(last, axis, up)  4.94 us
    add x4, other arithmetic, scatter_window(): current + combined[window]  4.46 us
  transfers between devices with their start and end apart: 6, of which 5 were waited for; matrix products, arithmetic and copies ran while one was open for 5% of the time, Pallas kernels for 0%

commit v1 on v0

v1 whole, which is shorter than its diff:
```python
import functools

import jax
import jax.numpy as jnp
from jax import lax
from jax.experimental import pallas as pl
from jax.experimental.pallas import tpu as pltpu
from jax.sharding import PartitionSpec as P

H = 4
HD = 32
QW = 32
KW = 128
HALO = 64
JIT = 16
EPSILON = 1e-05
MESH = pl.DeviceIdType.MESH
F32 = jnp.float32
BF16 = jnp.bfloat16


def dot(a, b, ca=1, cb=0, precision=None):
    return lax.dot_general(
        a, b, (((ca,), (cb,)), ((), ())), preferred_element_type=F32, precision=precision
    )


def iota(shape, dim):
    return lax.broadcasted_iota(jnp.int32, shape, dim)


def layer_norm(values):
    center = values - jnp.mean(values, axis=-1, keepdims=True)
    variance = jnp.mean(center * center, axis=-1, keepdims=True)
    inverse = 1.0 / jnp.sqrt(variance + EPSILON)
    return (center * inverse, inverse)


def sigmoid(x):
    return 0.5 + 0.5 * jnp.tanh(0.5 * x)


def per_head(values, lane_head):
    total = values[0:QW]
    for h in range(1, H):
        total = jnp.where(lane_head == h, values[h * QW : (h + 1) * QW], total)
    return total


def kernel(
    n_seq,
    n_smp,
    n_rep,
    x_hbm,
    counts_ref,
    shift_ref,
    pair_hbm,
    pw_hbm,
    bw_ref,
    ow_hbm,
    tw_hbm,
    tg_hbm,
    single_out,
    pair_out,
    token_out,
    project_out,
    x_ext,
    pair,
    pw,
    ow,
    tw,
    tg,
    nh,
    nf,
    inv,
    q_s,
    k_s,
    v_s,
    gate_s,
    bias_s,
    prob_s,
    hid_s,
    sg_s,
    hg_s,
    da_s,
    dg_s,
    dq_s,
    dk_s,
    dv_s,
    kv_win,
    acc,
    lacc,
    psend32,
    psend,
    precv,
    tsend,
    t1,
    t2,
    t3,
    wsend,
    w1,
    w2,
    w3,
    hsend,
    hrecv,
    load_sem,
    halo_send,
    halo_recv,
    back_send,
    back_recv,
    pair_send_sem,
    pair_recv_sem,
    t_send_q,
    t_recv_q,
    t_send_z,
    t_recv_z,
    t_send_f,
    t_recv_f,
    w_send_q,
    w_recv_q,
    w_send_z,
    w_recv_z,
    w_send_f,
    w_recv_f,
):
    samples, ext, width = x_ext.shape
    atoms = ext - 2 * HALO
    windows = bias_s.shape[0]
    nq = n_smp * n_rep
    z = lax.axis_index("seq")
    me_q = lax.axis_index("smp") * n_rep + lax.axis_index("rep")
    scale = HD ** (-0.5)

    def seq_peer(offset):
        return {"seq": lax.rem(z + offset, n_seq)}

    def quarter_peer(offset):
        other = lax.rem(me_q + offset, nq)
        return other, {"smp": other // n_rep, "rep": lax.rem(other, n_rep)}

    own = slice(HALO, HALO + atoms)
    loads = [
        pltpu.make_async_copy(source, target, load_sem.at[i])
        for i, (source, target) in enumerate(
            [
                (x_hbm, x_ext.at[:, HALO : HALO + atoms, :]),
                (pw_hbm, pw),
                (pair_hbm, pair),
                (ow_hbm, ow),
                (tw_hbm, tw),
                (tg_hbm, tg),
            ]
        )
    ]
    for load in loads:
        load.start()

    barrier = pltpu.get_barrier_semaphore()
    for k in range(1, n_seq):
        pl.semaphore_signal(barrier, inc=1, device_id=seq_peer(k), device_id_type=MESH)
    for k in range(1, nq):
        pl.semaphore_signal(barrier, inc=1, device_id=quarter_peer(k)[1], device_id_type=MESH)
    pl.semaphore_wait(barrier, n_seq - 1 + nq - 1)

    up = pltpu.make_async_remote_copy(
        src_ref=x_hbm.at[:, atoms - HALO : atoms, :],
        dst_ref=x_ext.at[:, 0:HALO, :],
        send_sem=halo_send.at[0],
        recv_sem=halo_recv.at[0],
        device_id={"seq": jnp.minimum(z + 1, n_seq - 1)},
        device_id_type=MESH,
    )
    down = pltpu.make_async_remote_copy(
        src_ref=x_hbm.at[:, 0:HALO, :],
        dst_ref=x_ext.at[:, HALO + atoms : ext, :],
        send_sem=halo_send.at[1],
        recv_sem=halo_recv.at[1],
        device_id={"seq": jnp.maximum(z - 1, 0)},
        device_id_type=MESH,
    )
    has_up = z < n_seq - 1
    has_down = z > 0

    @pl.when(has_up)
    def _():
        up.start()

    @pl.when(has_down)
    def _():
        down.start()

    @pl.when(z == 0)
    def _():
        x_ext[:, 0:HALO, :] = jnp.zeros((samples, HALO, width), BF16)

    @pl.when(z == n_seq - 1)
    def _():
        x_ext[:, HALO + atoms : ext, :] = jnp.zeros((samples, HALO, width), BF16)

    loads[0].wait()
    loads[1].wait()
    rows = samples * atoms
    normed, inverse = layer_norm(x_ext[:, own, :].reshape(rows, width).astype(F32))
    nf[...] = normed.reshape(samples, atoms, width)
    inv[...] = inverse.reshape(samples, atoms, 1)
    half = normed.astype(BF16)
    nh[:, own, :] = half.reshape(samples, atoms, width)
    q_s[...] = dot(half, pw[0]).astype(BF16).reshape(samples, atoms, width)
    k_s[:, own, :] = dot(half, pw[1]).astype(BF16).reshape(samples, atoms, width)
    v_s[:, own, :] = dot(half, pw[2]).astype(BF16).reshape(samples, atoms, width)
    gate_s[...] = sigmoid(dot(half, pw[3])).reshape(samples, atoms, width)

    pairs_wide = pair.shape[1]
    group = 16
    deep = group * pairs_wide
    bw = bw_ref[...]
    terms = []
    rest = bw
    for _ in range(3):
        term = rest.astype(BF16)
        terms.append(term)
        rest = rest - term.astype(F32)
    spread = (
        jnp.bitwise_and(iota((pairs_wide, deep), 1), pairs_wide - 1) == iota((pairs_wide, deep), 0)
    ).astype(BF16)
    diagonal = iota((group, deep), 1) // pairs_wide == iota((group, deep), 0)
    mixer = []
    for term in terms:
        line = dot(term, spread, 0, 0)
        for h in range(H):
            mixer.append(
                jnp.where(diagonal, jnp.broadcast_to(line[h : h + 1], (group, deep)), 0.0)
            )
    mixer = jnp.concatenate(mixer, axis=0).astype(BF16)
    loads[2].wait()
    key_at = iota((1, KW), 1)
    for w in range(windows):
        first = z * atoms + QW * w - (KW - QW) // 2 + shift_ref[w]
        key_global = first + key_at
        mask = jnp.where((key_global >= 0) & (key_global < n_seq * atoms), 0.0, -1e30)
        for g in range(QW // group):
            stack = jnp.concatenate(
                [pair[w, :, (g * group + r) * KW : (g * group + r + 1) * KW] for r in range(group)],
                axis=0,
            )
            mixed = dot(mixer, stack)
            part = H * group
            mixed = mixed[0:part] + (mixed[part : 2 * part] + mixed[2 * part : 3 * part])
            for h in range(H):
                bias_s[w, h * QW + g * group : h * QW + (g + 1) * group, :] = (
                    mixed[h * group : (h + 1) * group] + mask
                )

    tokens = counts_ref.shape[1]
    counts = counts_ref[...].astype(F32)
    before = (iota((tokens, tokens), 0) < iota((tokens, tokens), 1)).astype(BF16)
    begins = dot(jnp.broadcast_to(counts, (8, tokens)).astype(BF16), before)[0:1]
    place = iota((atoms, tokens), 0).astype(F32)
    member32 = jnp.where((place >= begins) & (place < begins + counts), 1.0, 0.0)
    per_atom = 1.0 / jnp.sum(member32 * counts, axis=1, keepdims=True)
    member = member32.astype(BF16)

    row_head = jnp.right_shift(iota((H * QW, width), 0), 5)
    lane_head = jnp.right_shift(iota((QW, width), 1), 5)
    head_mask = (row_head == jnp.right_shift(iota((H * QW, width), 1), 5)).astype(BF16)

    lacc[...] = jnp.zeros_like(lacc)

    @pl.when(has_down)
    def _():
        up.wait_recv()

    @pl.when(has_up)
    def _():
        down.wait_recv()

    for side in (slice(0, HALO), slice(HALO + atoms, ext)):
        side_normed, _ = layer_norm(x_ext[:, side, :].reshape(samples * HALO, width).astype(F32))
        side_half = side_normed.astype(BF16)
        nh[:, side, :] = side_half.reshape(samples, HALO, width)
        k_s[:, side, :] = dot(side_half, pw[1]).astype(BF16).reshape(samples, HALO, width)
        v_s[:, side, :] = dot(side_half, pw[2]).astype(BF16).reshape(samples, HALO, width)
    for i in (3, 4, 5):
        loads[i].wait()

    moves = []
    weights = []
    for w in range(windows):
        moved = jnp.full((1, width), shift_ref[w], jnp.int32)
        moves.append((moved < 0, moved == 0))
        weights.append(
            [jnp.where(moved == JIT * step, 1.0, 0.0).astype(BF16) for step in (-1, 0, 1)]
        )

    def window_of(ref, s, w):
        total = None
        for step in range(3):
            at = w * QW + step * JIT
            term = ref[s, at : at + KW, :] * weights[w][step]
            total = term if total is None else total + term
        return total

    def moved_back(values, w):
        blank = jnp.zeros((JIT, width), F32)
        low, middle = moves[w]
        return jnp.where(
            low,
            jnp.concatenate([values, blank, blank], axis=0),
            jnp.where(
                middle,
                jnp.concatenate([blank, values, blank], axis=0),
                jnp.concatenate([blank, blank, values], axis=0),
            ),
        )

    def spread_heads(values):
        return jnp.concatenate([values] * H, axis=0) * head_mask

    chunk = 256
    token_width = tw.shape[1]

    def forward(s, carry):
        parts = []
        for w in range(windows):
            keys = window_of(k_s, s, w)
            values = window_of(v_s, s, w)
            kv_win[s, w, 0] = keys
            kv_win[s, w, 1] = values
            queries = spread_heads(q_s[s, w * QW : (w + 1) * QW, :])
            scores = dot(queries, keys, 1, 1) * scale + bias_s[w]
            expo = jnp.exp(scores - jnp.max(scores, axis=-1, keepdims=True))
            probs = expo * (1.0 / jnp.sum(expo, axis=-1, keepdims=True))
            prob_s[s, w] = probs
            parts.append(per_head(dot(probs.astype(BF16), values), lane_head))
        attended = jnp.concatenate(parts, axis=0)
        gate = gate_s[s]
        gated = (gate * attended).astype(BF16)
        hidden = (x_ext[s, own, :].astype(F32) + dot(gated, ow[...])).astype(BF16)
        hid_s[s] = hidden
        hidden_grad = jnp.zeros((atoms, width), F32)
        for b in range(token_width // chunk):
            columns = slice(b * chunk, (b + 1) * chunk)
            weight = tw[:, columns]
            preact = dot(hidden, weight)
            picked = dot(member, tg[s, :, columns]) * per_atom
            sigma = sigmoid(preact)
            slope = (picked * (sigma * (1.0 + preact * (1.0 - sigma)))).astype(BF16)
            sg_s[s, :, columns] = slope
            hidden_grad = hidden_grad + dot(slope, weight, 1, 1)
        hg_s[s] = hidden_grad
        gated_grad = dot(hidden_grad.astype(BF16), ow[...], 1, 1)
        da_s[s] = (gated_grad * gate).astype(BF16)
        dg_s[s] = (gated_grad * attended * gate * (1.0 - gate)).astype(BF16)
        return carry

    lax.fori_loop(0, samples, forward, 0)

    def send_pieces(source, slots, send, recv):
        size = slots.shape[1]
        copies = []
        for k in range(1, nq):
            other, where = quarter_peer(k)
            copies.append(
                pltpu.make_async_remote_copy(
                    src_ref=source.at[pl.ds(pl.multiple_of(other * size, 16), size), :],
                    dst_ref=slots.at[me_q],
                    send_sem=send.at[k],
                    recv_sem=recv.at[k],
                    device_id=where,
                    device_id_type=MESH,
                )
            )
        for copy in copies:
            copy.start()
        slots[me_q] = source[pl.ds(pl.multiple_of(me_q * size, 16), size), :]
        return copies

    def send_along(first, slots, send, recv, arrived):
        for copy in arrived:
            copy.wait_recv()
        total = first[0].astype(F32)
        for i in range(1, nq):
            total = total + first[i].astype(F32)
        slots[z] = total.astype(BF16)
        copies = [
            pltpu.make_async_remote_copy(
                src_ref=slots.at[z],
                dst_ref=slots.at[z],
                send_sem=send.at[k],
                recv_sem=recv.at[k],
                device_id=seq_peer(k),
                device_id_type=MESH,
            )
            for k in range(1, n_seq)
        ]
        for copy in copies:
            copy.start()
        return copies

    def send_back(second, target, send, recv, arrived):
        for copy in arrived:
            copy.wait_recv()
        size = second.shape[1]
        total = second[0].astype(F32)
        for i in range(1, n_seq):
            total = total + second[i].astype(F32)
        mine = pl.ds(pl.multiple_of(me_q * size, 16), size)
        target[mine, :] = total.astype(BF16)
        copies = [
            pltpu.make_async_remote_copy(
                src_ref=target.at[mine, :],
                dst_ref=target.at[mine, :],
                send_sem=send.at[k],
                recv_sem=recv.at[k],
                device_id=quarter_peer(k)[1],
                device_id_type=MESH,
            )
            for k in range(1, nq)
        ]
        for copy in copies:
            copy.start()
        return copies

    all_hidden = hid_s[...].reshape(rows, width)
    for b in range(token_width // chunk):
        part = dot(all_hidden, sg_s[:, :, b * chunk : (b + 1) * chunk].reshape(rows, chunk), 0, 0)
        for i in range(chunk // width):
            at = (b * (chunk // width) + i) * width
            tsend[at : at + width, :] = part[:, i * width : (i + 1) * width].astype(BF16)
    token_pieces = send_pieces(tsend, t1, t_send_q, t_recv_q)

    def backward(s, carry):
        acc[...] = jnp.zeros_like(acc)
        parts = []
        for w in range(windows):
            keys = kv_win[s, w, 0]
            values = kv_win[s, w, 1]
            queries = spread_heads(q_s[s, w * QW : (w + 1) * QW, :])
            upstream = spread_heads(da_s[s, w * QW : (w + 1) * QW, :])
            probs = prob_s[s, w]
            prob_grad = dot(upstream, values, 1, 1)
            weighted = probs * prob_grad
            logit_grad = weighted - probs * jnp.sum(weighted, axis=-1, keepdims=True)
            lacc[w] += logit_grad
            logit_half = logit_grad.astype(BF16)
            parts.append(per_head(dot(logit_half, keys), lane_head))
            reach = slice(w * QW, w * QW + KW + QW)
            acc[0, reach, :] += moved_back(dot(logit_half, queries, 0, 0), w)
            acc[1, reach, :] += moved_back(dot(probs.astype(BF16), upstream, 0, 0), w)
        dq_s[s] = (jnp.concatenate(parts, axis=0) * scale).astype(BF16)
        dk_s[s] = (acc[0] * scale).astype(BF16)
        dv_s[s] = acc[1].astype(BF16)
        return carry

    lax.fori_loop(0, samples // 2, backward, 0)
    token_along = send_along(t1, t2, t_send_z, t_recv_z, token_pieces)
    lax.fori_loop(samples // 2, samples, backward, 0)

    for i, side in enumerate((slice(HALO + atoms, ext), slice(0, HALO))):
        side_grad = dot(dk_s[:, side, :].reshape(samples * HALO, width), pw[1], 1, 1) + dot(
            dv_s[:, side, :].reshape(samples * HALO, width), pw[2], 1, 1
        )
        hsend[i] = side_grad.astype(BF16).reshape(samples, HALO, width)
    back_up = pltpu.make_async_remote_copy(
        src_ref=hsend.at[0],
        dst_ref=hrecv.at[0],
        send_sem=back_send.at[0],
        recv_sem=back_recv.at[0],
        device_id={"seq": jnp.minimum(z + 1, n_seq - 1)},
        device_id_type=MESH,
    )
    back_down = pltpu.make_async_remote_copy(
        src_ref=hsend.at[1],
        dst_ref=hrecv.at[1],
        send_sem=back_send.at[1],
        recv_sem=back_recv.at[1],
        device_id={"seq": jnp.maximum(z - 1, 0)},
        device_id_type=MESH,
    )

    @pl.when(has_up)
    def _():
        back_up.start()

    @pl.when(has_down)
    def _():
        back_down.start()

    @pl.when(z == 0)
    def _():
        hrecv[0] = jnp.zeros((samples, HALO, width), BF16)

    @pl.when(z == n_seq - 1)
    def _():
        hrecv[1] = jnp.zeros((samples, HALO, width), BF16)

    own_half = nh[:, own, :].reshape(rows, width)
    all_half = nh[...].reshape(samples * ext, width)
    wsend[0:width, :] = dot(own_half, dq_s[...].reshape(rows, width), 0, 0).astype(BF16)
    wsend[width : 2 * width, :] = dot(
        all_half, dk_s[...].reshape(samples * ext, width), 0, 0
    ).astype(BF16)
    wsend[2 * width : 3 * width, :] = dot(
        all_half, dv_s[...].reshape(samples * ext, width), 0, 0
    ).astype(BF16)
    wsend[3 * width : 4 * width, :] = dot(own_half, dg_s[...].reshape(rows, width), 0, 0).astype(
        BF16
    )
    project_pieces = send_pieces(wsend, w1, w_send_q, w_recv_q)

    rows_q = QW // nq
    for j in range(nq):
        for w in range(windows):
            for h in range(H):
                at = (w * H + h) * rows_q
                psend32[j, at : at + rows_q, :] = lacc[
                    w, h * QW + j * rows_q : h * QW + (j + 1) * rows_q, :
                ]
    psend[...] = psend32[...].astype(BF16)
    pair_copies = []
    for k in range(1, nq):
        other, where = quarter_peer(k)
        pair_copies.append(
            pltpu.make_async_remote_copy(
                src_ref=psend.at[other],
                dst_ref=precv.at[me_q],
                send_sem=pair_send_sem.at[k],
                recv_sem=pair_recv_sem.at[k],
                device_id=where,
                device_id_type=MESH,
            )
        )
    for copy in pair_copies:
        copy.start()
    precv[me_q] = psend[me_q]

    token_back = send_back(t2, t3, t_send_f, t_recv_f, token_along)

    own_grad = (
        dot(dq_s[...].reshape(rows, width), pw[0], 1, 1)
        + dot(dk_s[:, own, :].reshape(rows, width), pw[1], 1, 1)
        + dot(dv_s[:, own, :].reshape(rows, width), pw[2], 1, 1)
        + dot(dg_s[...].reshape(rows, width), pw[3], 1, 1)
    ).reshape(samples, atoms, width)

    project_along = send_along(w1, w2, w_send_z, w_recv_z, project_pieces)

    @pl.when(has_down)
    def _():
        back_up.wait_recv()

    @pl.when(has_up)
    def _():
        back_down.wait_recv()

    arrived = jnp.concatenate([hrecv[0], hrecv[1]], axis=1).astype(F32)
    normed_grad = own_grad + arrived
    normed = nf[...]
    ln_grad = inv[...] * (
        normed_grad
        - jnp.mean(normed_grad, axis=-1, keepdims=True)
        - normed * jnp.mean(normed_grad * normed, axis=-1, keepdims=True)
    )
    single_out[...] = (hg_s[...] + ln_grad).astype(BF16)

    for copy in pair_copies:
        copy.wait_recv()
    heads = precv[0].astype(F32)
    for i in range(1, nq):
        heads = heads + precv[i].astype(F32)
    tall, deep = rows_q * pairs_wide, H * rows_q
    lift = (
        jnp.bitwise_and(iota((tall, pairs_wide), 0), pairs_wide - 1) == iota((tall, pairs_wide), 1)
    ).astype(F32)
    widen = (iota((H, deep), 1) // rows_q == iota((H, deep), 0)).astype(F32)
    highest = lax.Precision.HIGHEST
    mix_back = dot(dot(lift, bw, precision=highest), widen, precision=highest)
    same = iota((tall, deep), 0) // pairs_wide == jnp.bitwise_and(
        iota((tall, deep), 1), rows_q - 1
    )
    mix_back = jnp.where(same, mix_back, 0.0)
    for w in range(windows):
        result = dot(mix_back, heads[w * deep : (w + 1) * deep], precision=highest).astype(BF16)
        for r in range(rows_q):
            pair_out[w, :, r * KW : (r + 1) * KW] = result[r * pairs_wide : (r + 1) * pairs_wide]

    project_back = send_back(w2, w3, w_send_f, w_recv_f, project_along)
    for copy in token_back:
        copy.wait_recv()
    for b in range(token_width // width):
        token_out[:, b * width : (b + 1) * width] = t3[b * width : (b + 1) * width, :].astype(F32)
    for copy in project_back:
        copy.wait_recv()
    for k in range(4):
        project_out[k] = w3[k * width : (k + 1) * width, :].astype(F32)

    for copies in (
        token_pieces,
        token_along,
        token_back,
        project_pieces,
        project_along,
        project_back,
        pair_copies,
    ):
        for copy in copies:
            copy.wait_send()

    @pl.when(has_up)
    def _():
        up.wait_send()
        back_up.wait_send()

    @pl.when(has_down)
    def _():
        down.wait_send()
        back_down.wait_send()


def solution(mesh):
    n_seq, n_smp, n_rep = (mesh.shape["seq"], mesh.shape["smp"], mesh.shape["rep"])
    nq = n_smp * n_rep

    def on_device(x, counts, shift, pair, pw, bw, ow, tw, tg):
        samples, atoms, width = x.shape
        ext = atoms + 2 * HALO
        windows, pairs_wide, spots = pair.shape
        token_width = tw.shape[1]
        any_space = pl.BlockSpec(memory_space=pl.ANY)
        vmem = pl.BlockSpec(memory_space=pltpu.VMEM)
        smem = pl.BlockSpec(memory_space=pltpu.SMEM)
        rows_q = QW // nq
        t_rows = token_width
        w_rows = 4 * width
        per_atom = (samples, atoms, width)
        per_ext = (samples, ext, width)
        square = (windows, H * QW, KW)
        dma = pltpu.SemaphoreType.DMA
        scratch = [
            pltpu.VMEM(per_ext, BF16),
            pltpu.VMEM(pair.shape, BF16),
            pltpu.VMEM(pw.shape, BF16),
            pltpu.VMEM(ow.shape, BF16),
            pltpu.VMEM(tw.shape, BF16),
            pltpu.VMEM(tg.shape, BF16),
            pltpu.VMEM(per_ext, BF16),
            pltpu.VMEM(per_atom, F32),
            pltpu.VMEM((samples, atoms, 1), F32),
            pltpu.VMEM(per_atom, BF16),
            pltpu.VMEM(per_ext, BF16),
            pltpu.VMEM(per_ext, BF16),
            pltpu.VMEM(per_atom, F32),
            pltpu.VMEM(square, F32),
            pltpu.VMEM((samples,) + square, F32),
            pltpu.VMEM(per_atom, BF16),
            pltpu.VMEM((samples, atoms, token_width), BF16),
            pltpu.VMEM(per_atom, F32),
            pltpu.VMEM(per_atom, BF16),
            pltpu.VMEM(per_atom, BF16),
            pltpu.VMEM(per_atom, BF16),
            pltpu.VMEM(per_ext, BF16),
            pltpu.VMEM(per_ext, BF16),
            pltpu.VMEM((samples, windows, 2, KW, width), BF16),
            pltpu.VMEM((2, ext, width), F32),
            pltpu.VMEM(square, F32),
            pltpu.VMEM((nq, windows * H * rows_q, KW), F32),
            pltpu.VMEM((nq, windows * H * rows_q, KW), BF16),
            pltpu.VMEM((nq, windows * H * rows_q, KW), BF16),
            pltpu.VMEM((t_rows, width), BF16),
            pltpu.VMEM((nq, t_rows // nq, width), BF16),
            pltpu.VMEM((n_seq, t_rows // nq, width), BF16),
            pltpu.VMEM((t_rows, width), BF16),
            pltpu.VMEM((w_rows, width), BF16),
            pltpu.VMEM((nq, w_rows // nq, width), BF16),
            pltpu.VMEM((n_seq, w_rows // nq, width), BF16),
            pltpu.VMEM((w_rows, width), BF16),
            pltpu.VMEM((2, samples, HALO, width), BF16),
            pltpu.VMEM((2, samples, HALO, width), BF16),
            dma((6,)),
        ]
        scratch += [dma((2,))] * 4
        scratch += [dma((nq,))] * 2
        scratch += [dma((n,)) for n in (nq, nq, n_seq, n_seq, nq, nq)] * 2
        return pl.pallas_call(
            functools.partial(kernel, n_seq, n_smp, n_rep),
            out_shape=(
                jax.ShapeDtypeStruct(x.shape, BF16),
                jax.ShapeDtypeStruct((windows, pairs_wide, spots // nq), BF16),
                jax.ShapeDtypeStruct(tw.shape, F32),
                jax.ShapeDtypeStruct(pw.shape, F32),
            ),
            in_specs=[
                any_space,
                vmem,
                smem,
                any_space,
                any_space,
                vmem,
                any_space,
                any_space,
                any_space,
            ],
            out_specs=(vmem,) * 4,
            scratch_shapes=scratch,
            compiler_params=pltpu.CompilerParams(
                collective_id=0, has_side_effects=True, vmem_limit_bytes=40 * 1024 * 1024
            ),
        )(x, counts, shift, pair, pw, bw, ow, tw, tg)

    in_specs = (
        P(("grp", "smp", "rep"), "seq", None),
        P(("grp", "seq"), None),
        P(("grp", "seq")),
        P(("grp", "seq"), None, None),
        P(),
        P(),
        P(),
        P(),
        P(("grp", "smp", "rep"), "seq", None),
    )
    out_specs = (
        P(("grp", "smp", "rep"), "seq", None),
        P(("grp", "seq"), None, ("smp", "rep")),
        P("grp", None),
        P("grp", None, None),
    )
    return jax.shard_map(
        on_device, mesh=mesh, in_specs=in_specs, out_specs=out_specs, check_vma=False
    )
```

time: 200 us -> 46.8 us (0.23)
  waiting for transfers between devices: 98.6 us -> 0 us
  Pallas kernels: 0 us -> 36.9 us
  local copies, waits for them, and re-layouts: 30.7 us -> 8.96 us
  matrix products: 20 us -> 0 us
  between operations: 16.1 us -> 0.67 us
  starting transfers between devices: 13.1 us -> 0 us
  other arithmetic: 12.8 us -> 0 us
  loops' own time: 7.96 us -> 0 us
    psum x1 -> x0, waiting for transfers between devices: 86.7 us -> none  [on_device(): lax.psum((token_part, project_part), ('seq', 'smp', 'rep'))]
    pallas_call x0 -> x1, Pallas kernels: none -> 36.9 us  [on_device(): pl.pallas_call(functools.partial(kernel, n_seq, n_smp, n_rep), out_shape=...]
    dot_general x16 -> x0, matrix products: 19.1 us -> none  [the longest x1 2.43 us: on_device(): jnp.einsum('sac,kcd->ksad', normed_half, project_weight, preferred_elemen...]
    ppermute x4 -> x0, starting transfers between devices: 13 us -> none  [the longest x2 6.81 us: from_behind(): lax.ppermute(value, axis, [(source, source + steps) for source in range(i...]
    ppermute x4 -> x0, waiting for transfers between devices: 11.9 us -> none  [the longest x2 6.97 us: from_behind(): lax.ppermute(value, axis, [(source, source + steps) for source in range(i...]
    dynamic_update_slice x8 -> x0, local copies, waits for them, and re-layouts: 11 us -> none  [scatter_window(): lax.dynamic_update_slice_in_dim(total, current + combined[window], start,...]
    another operation x1 -> x0, loops' own time: 7.96 us -> none  [on_device(): lax.fori_loop(0, windows, scatter_window, jnp.zeros((samples, atoms + 2 *...]
    add x5 -> x0, other arithmetic: 4.47 us -> none  [the longest x4 4.46 us: scatter_window(): current + combined[window]]
  transfers between devices with their start and end apart: 6 -> 0, of which waited for: 5 -> 0; matrix products, arithmetic and copies ran while one was open for 5% -> 0% of each run, Pallas kernels for 0% -> 0%
where the time goes in v1:
time: 46.8 us; the launch traced here: 46.5 us
  Pallas kernels  36.9 us (79%)
  local copies, waits for them, and re-layouts  8.96 us (19%)
  between operations  0.67 us (1%)
    pallas_call x1, Pallas kernels, on_device(): pl.pallas_call(functools.partial(kernel, n_seq, n_smp, n_rep), out_shape=...  36.9 us
    unnamed x21, local copies, waits for them, and re-layouts  8.96 us

profile of v1, /device:TPU:0, one launch (start us, length us, event | category | flops | bytes accessed | tf_op | source)
XLA Modules:
  0.0 46.5 jit_solution(3038332540886785430)
XLA Ops:
  0.6 0.0 copy-start.7
  0.6 0.0 copy-start.6
  0.7 0.8 %copy.13.bw_ref = f32[16,4]{1,0:T(8,128)S(1)} copy(f32[16,4]{0,1:T(4,128)} %param.14) | data formatting | bytes 512 | tf_op args[5]
  1.4 0.0 copy-done.7
  1.4 0.0 copy-done.6
  1.4 0.0 copy-start
  1.4 1.0 %copy-done = bf16[4,16,4096]{2,1,0:T(8,128)(2,1)S(1)} copy-done((bf16[4,16,4096]{2,1,0:T(8,128)(2,1)S(1)}, bf16[4,16,4096]{2,1,0:T(8,128)(2,1)}, u32[]{:S(2)}) %copy-start) | copy-done | bytes 524312
  2.5 0.0 copy-start.1
  2.5 0.9 %copy-done.1 = bf16[128,768]{1,0:T(8,128)(2,1)S(1)} copy-done((bf16[128,768]{1,0:T(8,128)(2,1)S(1)}, bf16[128,768]{1,0:T(8,128)(2,1)}, u32[]{:S(2)}) %copy-start.1) | copy-done | bytes 196632
  3.4 0.0 copy-start.2
  3.4 0.9 %copy-done.2 = bf16[4,128,128]{2,1,0:T(8,128)(2,1)S(1)} copy-done((bf16[4,128,128]{2,1,0:T(8,128)(2,1)S(1)}, bf16[4,128,128]{2,1,0:T(8,128)(2,1)}, u32[]{:S(2)}) %copy-start.2) | copy-done | bytes 131096
  4.3 0.0 copy-start.3
  4.3 0.9 %copy-done.3 = bf16[4,128,128]{2,1,0:T(8,128)(2,1)S(1)} copy-done((bf16[4,128,128]{2,1,0:T(8,128)(2,1)S(1)}, bf16[4,128,128]{2,1,0:T(8,128)(2,1)}, u32[]{:S(2)}) %copy-start.3) | copy-done | bytes 131096
  5.2 0.0 copy-start.4
  5.2 0.9 %copy-done.4 = bf16[4,16,768]{2,1,0:T(8,128)(2,1)S(1)} copy-done((bf16[4,16,768]{2,1,0:T(8,128)(2,1)S(1)}, bf16[4,16,768]{2,1,0:T(8,128)(2,1)}, u32[]{:S(2)}) %copy-start.4) | copy-done | bytes 98328
  6.1 0.0 copy-start.5
  6.1 0.8 %copy-done.5 = bf16[128,128]{1,0:T(8,128)(2,1)S(1)} copy-done((bf16[128,128]{1,0:T(8,128)(2,1)S(1)}, bf16[128,128]{1,0:T(8,128)(2,1)}, u32[]{:S(2)}) %copy-start.5) | copy-done | bytes 32792
  6.9 36.9 %shard_map.120 = (bf16[4,128,128]{2,1,0:T(8,128)(2,1)S(1)}, bf16[4,16,1024]{2,1,0:T(8,128)(2,1)S(1)}, f32[128,768]{1,0:T(8,128)S(1)}, f32[4,128,128]{2,1,0:T(8,128)S(1)}) custom-call(bf16[4,128,128]{2,1,0:T(8,128)(2,1)S(1)} %copy-done.2, s32[1,16]{1,0:T(1,128)S(1)} %copy-done.6, s32[4]{0:T(128)S(1)} %copy-done.7, bf16[4,16,4096]{2,1,0:T(8,128)(2,1)S(1)} %copy-done, ...), custom_call_target="tpu_custom_call" | custom-call | tf_op jit(solution)/shard_map/pallas_call | solution.py:684
  43.7 0.7 %copy.18 = bf16[4,128,128]{2,1,0:T(8,128)(2,1)} copy(bf16[4,128,128]{2,1,0:T(8,128)(2,1)S(1)} %get-tuple-element.8) | data formatting | bytes 262144
  44.4 0.7 %copy.19 = bf16[4,16,1024]{2,1,0:T(8,128)(2,1)} copy(bf16[4,16,1024]{2,1,0:T(8,128)(2,1)S(1)} %get-tuple-element.9) | data formatting | bytes 262144
  45.0 0.7 %copy.20 = f32[128,768]{1,0:T(8,128)} copy(f32[128,768]{1,0:T(8,128)S(1)} %get-tuple-element.10) | data formatting | bytes 786432
  45.8 0.7 %copy.21 = f32[4,128,128]{2,1,0:T(8,128)} copy(f32[4,128,128]{2,1,0:T(8,128)S(1)} %get-tuple-element.11) | data formatting | bytes 524288
Async XLA Ops:
  0.6 0.8 %copy-start.7 = (s32[4]{0:T(128)S(1)}, s32[4]{0:T(128)}, u32[]{:S(2)}) copy-start(s32[4]{0:T(128)} %shift_ref.1) | copy-start | bytes 52
  0.6 0.8 %copy-start.6 = (s32[1,16]{1,0:T(1,128)S(1)}, s32[1,16]{1,0:T(1,128)}, u32[]{:S(2)}) copy-start(s32[1,16]{1,0:T(1,128)} %counts_ref.1) | copy-start | bytes 196
  1.4 1.0 %copy-start = (bf16[4,16,4096]{2,1,0:T(8,128)(2,1)S(1)}, bf16[4,16,4096]{2,1,0:T(8,128)(2,1)}, u32[]{:S(2)}) copy-start(bf16[4,16,4096]{2,1,0:T(8,128)(2,1)} %pair_hbm.1) | copy-start | bytes 1572868
  2.5 0.9 %copy-start.1 = (bf16[128,768]{1,0:T(8,128)(2,1)S(1)}, bf16[128,768]{1,0:T(8,128)(2,1)}, u32[]{:S(2)}) copy-start(bf16[128,768]{1,0:T(8,128)(2,1)} %tw_hbm.1) | copy-start | bytes 589828
  3.4 0.9 %copy-start.2 = (bf16[4,128,128]{2,1,0:T(8,128)(2,1)S(1)}, bf16[4,128,128]{2,1,0:T(8,128)(2,1)}, u32[]{:S(2)}) copy-start(bf16[4,128,128]{2,1,0:T(8,128)(2,1)} %x_hbm.1) | copy-start | bytes 393220
  4.3 0.9 %copy-start.3 = (bf16[4,128,128]{2,1,0:T(8,128)(2,1)S(1)}, bf16[4,128,128]{2,1,0:T(8,128)(2,1)}, u32[]{:S(2)}) copy-start(bf16[4,128,128]{2,1,0:T(8,128)(2,1)} %pw_hbm.1) | copy-start | bytes 393220
  5.2 0.9 %copy-start.4 = (bf16[4,16,768]{2,1,0:T(8,128)(2,1)S(1)}, bf16[4,16,768]{2,1,0:T(8,128)(2,1)}, u32[]{:S(2)}) copy-start(bf16[4,16,768]{2,1,0:T(8,128)(2,1)} %tg_hbm.1) | copy-start | bytes 294916
  6.1 0.8 %copy-start.5 = (bf16[128,128]{1,0:T(8,128)(2,1)S(1)}, bf16[128,128]{1,0:T(8,128)(2,1)}, u32[]{:S(2)}) copy-start(bf16[128,128]{1,0:T(8,128)(2,1)} %ow_hbm.1) | copy-start | bytes 98308

commit v2 on v1

--- a/solution.py
+++ b/solution.py
@@ -79,14 +79,12 @@
     gate_s,
     bias_s,
     prob_s,
-    hid_s,
+    att_s,
     sg_s,
     hg_s,
     da_s,
-    dg_s,
-    dq_s,
-    dk_s,
-    dv_s,
+    dqg_s,
+    dkv_s,
     kv_win,
     acc,
     lacc,
@@ -144,7 +142,10 @@
         for i, (source, target) in enumerate(
             [
                 (x_hbm, x_ext.at[:, HALO : HALO + atoms, :]),
-                (pw_hbm, pw),
+                (pw_hbm.at[0], pw.at[:, 0:width]),
+                (pw_hbm.at[3], pw.at[:, width : 2 * width]),
+                (pw_hbm.at[1], pw.at[:, 2 * width : 3 * width]),
+                (pw_hbm.at[2], pw.at[:, 3 * width : 4 * width]),
                 (pair_hbm, pair),
                 (ow_hbm, ow),
                 (tw_hbm, tw),
@@ -197,18 +198,20 @@
     def _():
         x_ext[:, HALO + atoms : ext, :] = jnp.zeros((samples, HALO, width), BF16)
 
-    loads[0].wait()
-    loads[1].wait()
+    for i in range(5):
+        loads[i].wait()
     rows = samples * atoms
     normed, inverse = layer_norm(x_ext[:, own, :].reshape(rows, width).astype(F32))
     nf[...] = normed.reshape(samples, atoms, width)
     inv[...] = inverse.reshape(samples, atoms, 1)
     half = normed.astype(BF16)
     nh[:, own, :] = half.reshape(samples, atoms, width)
-    q_s[...] = dot(half, pw[0]).astype(BF16).reshape(samples, atoms, width)
-    k_s[:, own, :] = dot(half, pw[1]).astype(BF16).reshape(samples, atoms, width)
-    v_s[:, own, :] = dot(half, pw[2]).astype(BF16).reshape(samples, atoms, width)
-    gate_s[...] = sigmoid(dot(half, pw[3])).reshape(samples, atoms, width)
+    wide = (samples, atoms, width)
+    projected = dot(half, pw[...])
+    q_s[...] = projected[:, 0:width].astype(BF16).reshape(wide)
+    gate_s[...] = sigmoid(projected[:, width : 2 * width]).reshape(wide)
+    k_s[:, own, :] = projected[:, 2 * width : 3 * width].astype(BF16).reshape(wide)
+    v_s[:, own, :] = projected[:, 3 * width :].astype(BF16).reshape(wide)
 
     pairs_wide = pair.shape[1]
     group = 16
@@ -226,13 +229,13 @@
     diagonal = iota((group, deep), 1) // pairs_wide == iota((group, deep), 0)
     mixer = []
     for term in terms:
-        line = dot(term, spread, 0, 0)
+        line = dot(term, spread)
         for h in range(H):
             mixer.append(
                 jnp.where(diagonal, jnp.broadcast_to(line[h : h + 1], (group, deep)), 0.0)
             )
     mixer = jnp.concatenate(mixer, axis=0).astype(BF16)
-    loads[2].wait()
+    loads[5].wait()
     key_at = iota((1, KW), 1)
     for w in range(windows):
         first = z * atoms + QW * w - (KW - QW) // 2 + shift_ref[w]
@@ -266,6 +269,19 @@
 
     lacc[...] = jnp.zeros_like(lacc)
 
+    rows_q = QW // nq
+    tall, flat = rows_q * pairs_wide, H * rows_q
+    lift = (
+        jnp.bitwise_and(iota((tall, pairs_wide), 0), pairs_wide - 1) == iota((tall, pairs_wide), 1)
+    ).astype(F32)
+    widen = (iota((H, flat), 1) // rows_q == iota((H, flat), 0)).astype(F32)
+    highest = lax.Precision.HIGHEST
+    mix_back = dot(dot(lift, bw, 1, 1, precision=highest), widen, precision=highest)
+    same = iota((tall, flat), 0) // pairs_wide == jnp.bitwise_and(
+        iota((tall, flat), 1), rows_q - 1
+    )
+    mix_back = jnp.where(same, mix_back, 0.0)
+
     @pl.when(has_down)
     def _():
         up.wait_recv()
@@ -278,9 +294,10 @@
         side_normed, _ = layer_norm(x_ext[:, side, :].reshape(samples * HALO, width).astype(F32))
         side_half = side_normed.astype(BF16)
         nh[:, side, :] = side_half.reshape(samples, HALO, width)
-        k_s[:, side, :] = dot(side_half, pw[1]).astype(BF16).reshape(samples, HALO, width)
-        v_s[:, side, :] = dot(side_half, pw[2]).astype(BF16).reshape(samples, HALO, width)
-    for i in (3, 4, 5):
+        side_kv = dot(side_half, pw[:, 2 * width :])
+        k_s[:, side, :] = side_kv[:, 0:width].astype(BF16).reshape(samples, HALO, width)
+        v_s[:, side, :] = side_kv[:, width:].astype(BF16).reshape(samples, HALO, width)
+    for i in (6, 7, 8):
         loads[i].wait()
 
     moves = []
@@ -319,41 +336,25 @@
     chunk = 256
     token_width = tw.shape[1]
 
-    def forward(s, carry):
-        parts = []
+    def attend(s, carry):
+        keys = [window_of(k_s, s, w) for w in range(windows)]
+        values = [window_of(v_s, s, w) for w in range(windows)]
+        queries = [spread_heads(q_s[s, w * QW : (w + 1) * QW, :]) for w in range(windows)]
+        scores = [dot(queries[w], keys[w], 1, 1) for w in range(windows)]
+        scores = [scores[w] * scale + bias_s[w] for w in range(windows)]
+        tops = [jnp.max(scores[w], axis=-1, keepdims=True) for w in range(windows)]
+        expos = [jnp.exp(scores[w] - tops[w]) for w in range(windows)]
+        sums = [jnp.sum(expos[w], axis=-1, keepdims=True) for w in range(windows)]
+        probs = [expos[w] * (1.0 / sums[w]) for w in range(windows)]
+        outs = [dot(probs[w].astype(BF16), values[w]) for w in range(windows)]
         for w in range(windows):
-            keys = window_of(k_s, s, w)
-            values = window_of(v_s, s, w)
-            kv_win[s, w, 0] = keys
-            kv_win[s, w, 1] = values
-            queries = spread_heads(q_s[s, w * QW : (w + 1) * QW, :])
-            scores = dot(queries, keys, 1, 1) * scale + bias_s[w]
-            expo = jnp.exp(scores - jnp.max(scores, axis=-1, keepdims=True))
-            probs = expo * (1.0 / jnp.sum(expo, axis=-1, keepdims=True))
-            prob_s[s, w] = probs
-            parts.append(per_head(dot(probs.astype(BF16), values), lane_head))
-        attended = jnp.concatenate(parts, axis=0)
-        gate = gate_s[s]
-        gated = (gate * attended).astype(BF16)
-        hidden = (x_ext[s, own, :].astype(F32) + dot(gated, ow[...])).astype(BF16)
-        hid_s[s] = hidden
-        hidden_grad = jnp.zeros((atoms, width), F32)
-        for b in range(token_width // chunk):
-            columns = slice(b * chunk, (b + 1) * chunk)
-            weight = tw[:, columns]
-            preact = dot(hidden, weight)
-            picked = dot(member, tg[s, :, columns]) * per_atom
-            sigma = sigmoid(preact)
-            slope = (picked * (sigma * (1.0 + preact * (1.0 - sigma)))).astype(BF16)
-            sg_s[s, :, columns] = slope
-            hidden_grad = hidden_grad + dot(slope, weight, 1, 1)
-        hg_s[s] = hidden_grad
-        gated_grad = dot(hidden_grad.astype(BF16), ow[...], 1, 1)
-        da_s[s] = (gated_grad * gate).astype(BF16)
-        dg_s[s] = (gated_grad * attended * gate * (1.0 - gate)).astype(BF16)
+            kv_win[s, w, 0] = keys[w]
+            kv_win[s, w, 1] = values[w]
+            prob_s[s, w] = probs[w]
+            att_s[s, w * QW : (w + 1) * QW, :] = per_head(outs[w], lane_head)
         return carry
 
-    lax.fori_loop(0, samples, forward, 0)
+    lax.fori_loop(0, samples, attend, 0)
 
     def send_pieces(source, slots, send, recv):
         size = slots.shape[1]
@@ -421,44 +422,79 @@
             copy.start()
         return copies
 
-    all_hidden = hid_s[...].reshape(rows, width)
+    attended = att_s[...].reshape(rows, width)
+    gate = gate_s[...].reshape(rows, width)
+    gated = (gate * attended).astype(BF16)
+    hidden = x_ext[:, own, :].reshape(rows, width).astype(F32) + dot(gated, ow[...])
+    hidden = hidden.astype(BF16)
     for b in range(token_width // chunk):
-        part = dot(all_hidden, sg_s[:, :, b * chunk : (b + 1) * chunk].reshape(rows, chunk), 0, 0)
-        for i in range(chunk // width):
-            at = (b * (chunk // width) + i) * width
-            tsend[at : at + width, :] = part[:, i * width : (i + 1) * width].astype(BF16)
+        columns = slice(b * chunk, (b + 1) * chunk)
+        preact = dot(hidden, tw[:, columns])
+        picked = jnp.concatenate(
+            [dot(member, tg[s, :, columns]) * per_atom for s in range(samples)], axis=0
+        )
+        sigma = sigmoid(preact)
+        sg_s[:, columns] = (picked * (sigma * (1.0 + preact * (1.0 - sigma)))).astype(BF16)
+    token_part = dot(hidden, sg_s[...], 0, 0)
+    for b in range(token_width // width):
+        tsend[b * width : (b + 1) * width, :] = token_part[:, b * width : (b + 1) * width].astype(
+            BF16
+        )
     token_pieces = send_pieces(tsend, t1, t_send_q, t_recv_q)
 
+    hidden_grad = dot(sg_s[...], tw[...], 1, 1)
+    hg_s[...] = hidden_grad.reshape(wide)
+    gated_grad = dot(hidden_grad.astype(BF16), ow[...], 1, 1)
+    gate = gate_s[...].reshape(rows, width)
+    attended = att_s[...].reshape(rows, width)
+    da_s[...] = (gated_grad * gate).astype(BF16).reshape(wide)
+    dqg_s[:, :, width:] = (
+        (gated_grad * attended * gate * (1.0 - gate)).astype(BF16).reshape(wide)
+    )
+
     def backward(s, carry):
+        each = range(windows)
+        values = [kv_win[s, w, 1] for w in each]
+        upstream = [spread_heads(da_s[s, w * QW : (w + 1) * QW, :]) for w in each]
+        prob_grad = [dot(upstream[w], values[w], 1, 1) for w in each]
+        value_grad = [dot(prob_s[s, w].astype(BF16), upstream[w], 0, 0) for w in each]
+        weighted = [prob_s[s, w] * prob_grad[w] for w in each]
+        sums = [jnp.sum(weighted[w], axis=-1, keepdims=True) for w in each]
+        logit_grad = [weighted[w] - prob_s[s, w] * sums[w] for w in each]
+        logit_half = [logit_grad[w].astype(BF16) for w in each]
+        query_grad = [dot(logit_half[w], kv_win[s, w, 0]) for w in each]
+        queries = [spread_heads(q_s[s, w * QW : (w + 1) * QW, :]) for w in each]
+        key_grad = [dot(logit_half[w], queries[w], 0, 0) for w in each]
         acc[...] = jnp.zeros_like(acc)
-        parts = []
-        for w in range(windows):
-            keys = kv_win[s, w, 0]
-            values = kv_win[s, w, 1]
-            queries = spread_heads(q_s[s, w * QW : (w + 1) * QW, :])
-            upstream = spread_heads(da_s[s, w * QW : (w + 1) * QW, :])
-            probs = prob_s[s, w]
-            prob_grad = dot(upstream, values, 1, 1)
-            weighted = probs * prob_grad
-            logit_grad = weighted - probs * jnp.sum(weighted, axis=-1, keepdims=True)
-            lacc[w] += logit_grad
-            logit_half = logit_grad.astype(BF16)
-            parts.append(per_head(dot(logit_half, keys), lane_head))
+        for w in each:
+            lacc[w] += logit_grad[w]
             reach = slice(w * QW, w * QW + KW + QW)
-            acc[0, reach, :] += moved_back(dot(logit_half, queries, 0, 0), w)
-            acc[1, reach, :] += moved_back(dot(probs.astype(BF16), upstream, 0, 0), w)
-        dq_s[s] = (jnp.concatenate(parts, axis=0) * scale).astype(BF16)
-        dk_s[s] = (acc[0] * scale).astype(BF16)
-        dv_s[s] = acc[1].astype(BF16)
+            acc[0, reach, :] += moved_back(key_grad[w], w)
+            acc[1, reach, :] += moved_back(value_grad[w], w)
+            dqg_s[s, w * QW : (w + 1) * QW, 0:width] = (
+                per_head(query_grad[w], lane_head) * scale
+            ).astype(BF16)
+        dkv_s[s, :, 0:width] = (acc[0] * scale).astype(BF16)
+        dkv_s[s, :, width:] = acc[1].astype(BF16)
         return carry
 
     lax.fori_loop(0, samples // 2, backward, 0)
     token_along = send_along(t1, t2, t_send_z, t_recv_z, token_pieces)
     lax.fori_loop(samples // 2, samples, backward, 0)
 
+    own_half = nh[:, own, :].reshape(rows, width)
+    all_half = nh[...].reshape(samples * ext, width)
+    query_gate = dot(own_half, dqg_s[...].reshape(rows, 2 * width), 0, 0).astype(BF16)
+    key_value = dot(all_half, dkv_s[...].reshape(samples * ext, 2 * width), 0, 0).astype(BF16)
+    wsend[0:width, :] = query_gate[:, 0:width]
+    wsend[width : 2 * width, :] = key_value[:, 0:width]
+    wsend[2 * width : 3 * width, :] = key_value[:, width:]
+    wsend[3 * width :, :] = query_gate[:, width:]
+    project_pieces = send_pieces(wsend, w1, w_send_q, w_recv_q)
+
     for i, side in enumerate((slice(HALO + atoms, ext), slice(0, HALO))):
-        side_grad = dot(dk_s[:, side, :].reshape(samples * HALO, width), pw[1], 1, 1) + dot(
-            dv_s[:, side, :].reshape(samples * HALO, width), pw[2], 1, 1
+        side_grad = dot(
+            dkv_s[:, side, :].reshape(samples * HALO, 2 * width), pw[:, 2 * width :], 1, 1
         )
         hsend[i] = side_grad.astype(BF16).reshape(samples, HALO, width)
     back_up = pltpu.make_async_remote_copy(
@@ -494,21 +530,6 @@
     def _():
         hrecv[1] = jnp.zeros((samples, HALO, width), BF16)
 
-    own_half = nh[:, own, :].reshape(rows, width)
-    all_half = nh[...].reshape(samples * ext, width)
-    wsend[0:width, :] = dot(own_half, dq_s[...].reshape(rows, width), 0, 0).astype(BF16)
-    wsend[width : 2 * width, :] = dot(
-        all_half, dk_s[...].reshape(samples * ext, width), 0, 0
-    ).astype(BF16)
-    wsend[2 * width : 3 * width, :] = dot(
-        all_half, dv_s[...].reshape(samples * ext, width), 0, 0
-    ).astype(BF16)
-    wsend[3 * width : 4 * width, :] = dot(own_half, dg_s[...].reshape(rows, width), 0, 0).astype(
-        BF16
-    )
-    project_pieces = send_pieces(wsend, w1, w_send_q, w_recv_q)
-
-    rows_q = QW // nq
     for j in range(nq):
         for w in range(windows):
             for h in range(H):
@@ -537,10 +558,8 @@
     token_back = send_back(t2, t3, t_send_f, t_recv_f, token_along)
 
     own_grad = (
-        dot(dq_s[...].reshape(rows, width), pw[0], 1, 1)
-        + dot(dk_s[:, own, :].reshape(rows, width), pw[1], 1, 1)
-        + dot(dv_s[:, own, :].reshape(rows, width), pw[2], 1, 1)
-        + dot(dg_s[...].reshape(rows, width), pw[3], 1, 1)
+        dot(dqg_s[...].reshape(rows, 2 * width), pw[:, 0 : 2 * width], 1, 1)
+        + dot(dkv_s[:, own, :].reshape(rows, 2 * width), pw[:, 2 * width :], 1, 1)
     ).reshape(samples, atoms, width)
 
     project_along = send_along(w1, w2, w_send_z, w_recv_z, project_pieces)
@@ -568,19 +587,8 @@
     heads = precv[0].astype(F32)
     for i in range(1, nq):
         heads = heads + precv[i].astype(F32)
-    tall, deep = rows_q * pairs_wide, H * rows_q
-    lift = (
-        jnp.bitwise_and(iota((tall, pairs_wide), 0), pairs_wide - 1) == iota((tall, pairs_wide), 1)
-    ).astype(F32)
-    widen = (iota((H, deep), 1) // rows_q == iota((H, deep), 0)).astype(F32)
-    highest = lax.Precision.HIGHEST
-    mix_back = dot(dot(lift, bw, precision=highest), widen, precision=highest)
-    same = iota((tall, deep), 0) // pairs_wide == jnp.bitwise_and(
-        iota((tall, deep), 1), rows_q - 1
-    )
-    mix_back = jnp.where(same, mix_back, 0.0)
     for w in range(windows):
-        result = dot(mix_back, heads[w * deep : (w + 1) * deep], precision=highest).astype(BF16)
+        result = dot(mix_back, heads[w * flat : (w + 1) * flat], precision=highest).astype(BF16)
         for r in range(rows_q):
             pair_out[w, :, r * KW : (r + 1) * KW] = result[r * pairs_wide : (r + 1) * pairs_wide]
 
@@ -639,7 +647,7 @@
         scratch = [
             pltpu.VMEM(per_ext, BF16),
             pltpu.VMEM(pair.shape, BF16),
-            pltpu.VMEM(pw.shape, BF16),
+            pltpu.VMEM((width, 4 * width), BF16),
             pltpu.VMEM(ow.shape, BF16),
             pltpu.VMEM(tw.shape, BF16),
             pltpu.VMEM(tg.shape, BF16),
@@ -652,14 +660,12 @@
             pltpu.VMEM(per_atom, F32),
             pltpu.VMEM(square, F32),
             pltpu.VMEM((samples,) + square, F32),
-            pltpu.VMEM(per_atom, BF16),
-            pltpu.VMEM((samples, atoms, token_width), BF16),
+            pltpu.VMEM(per_atom, F32),
+            pltpu.VMEM((samples * atoms, token_width), BF16),
             pltpu.VMEM(per_atom, F32),
             pltpu.VMEM(per_atom, BF16),
-            pltpu.VMEM(per_atom, BF16),
-            pltpu.VMEM(per_atom, BF16),
-            pltpu.VMEM(per_ext, BF16),
-            pltpu.VMEM(per_ext, BF16),
+            pltpu.VMEM((samples, atoms, 2 * width), BF16),
+            pltpu.VMEM((samples, ext, 2 * width), BF16),
             pltpu.VMEM((samples, windows, 2, KW, width), BF16),
             pltpu.VMEM((2, ext, width), F32),
             pltpu.VMEM(square, F32),
@@ -676,7 +682,7 @@
             pltpu.VMEM((w_rows, width), BF16),
             pltpu.VMEM((2, samples, HALO, width), BF16),
             pltpu.VMEM((2, samples, HALO, width), BF16),
-            dma((6,)),
+            dma((9,)),
         ]
         scratch += [dma((2,))] * 4
         scratch += [dma((nq,))] * 2
@@ -703,9 +709,9 @@
             out_specs=(vmem,) * 4,
             scratch_shapes=scratch,
             compiler_params=pltpu.CompilerParams(
-                collective_id=0, has_side_effects=True, vmem_limit_bytes=40 * 1024 * 1024
+                collective_id=0, has_side_effects=True, vmem_limit_bytes=60 * 1024 * 1024
             ),
-        )(x, counts, shift, pair, pw, bw, ow, tw, tg)
+        )(x, counts, shift, pair, pw, bw.T, ow, tw, tg)
 
     in_specs = (
         P(("grp", "smp", "rep"), "seq", None),

time: 46.8 us -> 37.8 us (0.81)
  Pallas kernels: 36.9 us -> 31.9 us
  local copies, waits for them, and re-layouts: 8.96 us -> 4.98 us
    pallas_call x1, Pallas kernels: 36.9 us -> 31.9 us  [on_device(): pl.pallas_call(functools.partial(kernel, n_seq, n_smp, n_rep), out_shape=...]
    unnamed x21 -> x8, local copies, waits for them, and re-layouts: 8.96 us -> 4.98 us
where the time goes in v2:
time: 37.8 us; the launch traced here: 37.6 us
  Pallas kernels  31.9 us (84%)
  local copies, waits for them, and re-layouts  4.98 us (13%)
  between operations  0.65 us (2%)
    pallas_call x1, Pallas kernels, on_device(): pl.pallas_call(functools.partial(kernel, n_seq, n_smp, n_rep), out_shape=...  31.9 us
    unnamed x8, local copies, waits for them, and re-layouts  4.98 us

profile of v2, /device:TPU:0, one launch (start us, length us, event | category | flops | bytes accessed | tf_op | source)
XLA Modules:
  0.0 37.6 jit_solution(3728680132261402332)
XLA Ops:
  0.6 31.9 %shard_map.120 = (bf16[4,128,128]{2,1,0:T(8,128)(2,1)}, bf16[4,16,1024]{2,1,0:T(8,128)(2,1)}, f32[128,768]{1,0:T(8,128)}, f32[4,128,128]{2,1,0:T(8,128)}) custom-call(bf16[4,128,128]{2,1,0:T(8,128)(2,1)} %x_hbm.1, s32[1,16]{1,0:T(1,128)} %counts_ref.1, s32[4]{0:T(128)} %shift_ref.1, bf16[4,16,4096]{2,1,0:T(8,128)(2,1)} %pair_hbm.1, ...), custom_call_target="tpu_custom_call" | custom-call | tf_op jit(solution)/shard_map/pallas_call | solution.py:690
  32.6 0.0 copy-start
  32.6 1.6 %copy.17 = bf16[4,128,128]{2,1,0:T(8,128)(2,1)} copy(bf16[4,128,128]{2,1,0:T(8,128)(2,1)} %get-tuple-element.8) | data formatting | bytes 262144
  34.2 1.6 %copy.18 = bf16[4,16,1024]{2,1,0:T(8,128)(2,1)} copy(bf16[4,16,1024]{2,1,0:T(8,128)(2,1)} %get-tuple-element.9) | data formatting | bytes 262144
  35.8 0.0 copy-done
  35.8 0.0 copy-start.1
  35.8 0.7 %copy.19 = f32[128,768]{1,0:T(8,128)} copy(f32[128,768]{1,0:T(8,128)S(1)} %copy-done) | data formatting | bytes 786432
  36.5 0.3 copy-done.1
  36.9 0.7 %copy.20 = f32[4,128,128]{2,1,0:T(8,128)} copy(f32[4,128,128]{2,1,0:T(8,128)S(1)} %copy-done.1) | data formatting | bytes 524288
Async XLA Ops:
  32.6 3.2 %copy-start = (f32[128,768]{1,0:T(8,128)S(1)}, f32[128,768]{1,0:T(8,128)}, u32[]{:S(2)}) copy-start(f32[128,768]{1,0:T(8,128)} %get-tuple-element.10) | copy-start | bytes 1179652
  35.8 1.1 %copy-start.1 = (f32[4,128,128]{2,1,0:T(8,128)S(1)}, f32[4,128,128]{2,1,0:T(8,128)}, u32[]{:S(2)}) copy-start(f32[4,128,128]{2,1,0:T(8,128)} %get-tuple-element.11) | copy-start | bytes 786436

commit v3 on v2

--- a/solution.py
+++ b/solution.py
@@ -478,9 +478,8 @@
         dkv_s[s, :, width:] = acc[1].astype(BF16)
         return carry
 
-    lax.fori_loop(0, samples // 2, backward, 0)
+    lax.fori_loop(0, samples, backward, 0)
     token_along = send_along(t1, t2, t_send_z, t_recv_z, token_pieces)
-    lax.fori_loop(samples // 2, samples, backward, 0)
 
     own_half = nh[:, own, :].reshape(rows, width)
     all_half = nh[...].reshape(samples * ext, width)
@@ -555,8 +554,6 @@
         copy.start()
     precv[me_q] = psend[me_q]
 
-    token_back = send_back(t2, t3, t_send_f, t_recv_f, token_along)
-
     own_grad = (
         dot(dqg_s[...].reshape(rows, 2 * width), pw[:, 0 : 2 * width], 1, 1)
         + dot(dkv_s[:, own, :].reshape(rows, 2 * width), pw[:, 2 * width :], 1, 1)
@@ -581,6 +578,8 @@
         - normed * jnp.mean(normed_grad * normed, axis=-1, keepdims=True)
     )
     single_out[...] = (hg_s[...] + ln_grad).astype(BF16)
+
+    token_back = send_back(t2, t3, t_send_f, t_recv_f, token_along)
 
     for copy in pair_copies:
         copy.wait_recv()

time: 37.8 us -> 36.6 us (0.968)
  Pallas kernels: 31.9 us -> 30.7 us
    pallas_call x1, Pallas kernels: 31.9 us -> 30.7 us  [on_device(): pl.pallas_call(functools.partial(kernel, n_seq, n_smp, n_rep), out_shape=...]
where the time goes in v3:
time: 36.6 us; the launch traced here: 36.4 us
  Pallas kernels  30.7 us (84%)
  local copies, waits for them, and re-layouts  4.98 us (14%)
  between operations  0.65 us (2%)
    pallas_call x1, Pallas kernels, on_device(): pl.pallas_call(functools.partial(kernel, n_seq, n_smp, n_rep), out_shape=...  30.7 us
    unnamed x8, local copies, waits for them, and re-layouts  4.98 us

profile of v3, /device:TPU:0, one launch (start us, length us, event | category | flops | bytes accessed | tf_op | source)
XLA Modules:
  0.0 36.4 jit_solution(8506429734072204974)
XLA Ops:
  0.6 30.7 %shard_map.120 = (bf16[4,128,128]{2,1,0:T(8,128)(2,1)}, bf16[4,16,1024]{2,1,0:T(8,128)(2,1)}, f32[128,768]{1,0:T(8,128)}, f32[4,128,128]{2,1,0:T(8,128)}) custom-call(bf16[4,128,128]{2,1,0:T(8,128)(2,1)} %x_hbm.1, s32[1,16]{1,0:T(1,128)} %counts_ref.1, s32[4]{0:T(128)} %shift_ref.1, bf16[4,16,4096]{2,1,0:T(8,128)(2,1)} %pair_hbm.1, ...), custom_call_target="tpu_custom_call" | custom-call | tf_op jit(solution)/shard_map/pallas_call | solution.py:689
  31.4 0.0 copy-start
  31.4 1.6 %copy.17 = bf16[4,128,128]{2,1,0:T(8,128)(2,1)} copy(bf16[4,128,128]{2,1,0:T(8,128)(2,1)} %get-tuple-element.8) | data formatting | bytes 262144
  33.0 1.6 %copy.18 = bf16[4,16,1024]{2,1,0:T(8,128)(2,1)} copy(bf16[4,16,1024]{2,1,0:T(8,128)(2,1)} %get-tuple-element.9) | data formatting | bytes 262144
  34.6 0.0 copy-done
  34.6 0.0 copy-start.1
  34.6 0.7 %copy.19 = f32[128,768]{1,0:T(8,128)} copy(f32[128,768]{1,0:T(8,128)S(1)} %copy-done) | data formatting | bytes 786432
  35.3 0.3 copy-done.1
  35.6 0.7 %copy.20 = f32[4,128,128]{2,1,0:T(8,128)} copy(f32[4,128,128]{2,1,0:T(8,128)S(1)} %copy-done.1) | data formatting | bytes 524288
Async XLA Ops:
  31.4 3.2 %copy-start = (f32[128,768]{1,0:T(8,128)S(1)}, f32[128,768]{1,0:T(8,128)}, u32[]{:S(2)}) copy-start(f32[128,768]{1,0:T(8,128)} %get-tuple-element.10) | copy-start | bytes 1179652
  34.6 1.1 %copy-start.1 = (f32[4,128,128]{2,1,0:T(8,128)S(1)}, f32[4,128,128]{2,1,0:T(8,128)}, u32[]{:S(2)}) copy-start(f32[4,128,128]{2,1,0:T(8,128)} %get-tuple-element.11) | copy-start | bytes 786436
